TPU v7x, 512 devices: a whole 4x8x8 slice. The times are simulated.
512 devices in a mesh: dp: 16 (over y, core), tensor: 32 (over z, x).
Axes of the slice: x: 4, y: 8, z: 8, core: 2. Of those that a mesh axis runs over, the one named last changes fastest.
Arguments:
- tokens: bfloat16 [2048, 4096], P('dp', 'tensor'), may hold values from -6 to 6
- gate_pre: bfloat16 [2048, 16384], P('dp', 'tensor'), may hold values from -6 to 6
- up_blocks: bfloat16 [32, 64, 128, 128], P('tensor'), may hold values from -0.125 to 0.125
- up_mask: int32 [32, 128], P(None, 'tensor'), may hold values from 0 to 1, as said below
- down_blocks: bfloat16 [32, 64, 128, 128], P('tensor'), may hold values from -0.0625 to 0.0625
- down_mask: int32 [128, 32], replicated, may hold values from 0 to 1, as said below
- down_owner: int32 [128], replicated, may hold values from 0 to 31, as said below
- cotangent: bfloat16 [2048, 4096], P('dp', 'tensor'), may hold values from -6 to 6
Outputs:
- mixed: bfloat16 [2048, 4096], P('dp', 'tensor')
- input_grad: bfloat16 [2048, 4096], P('dp', 'tensor')
- gate_grad: bfloat16 [2048, 16384], P('dp', 'tensor')
- up_grad: bfloat16 [32, 64, 128, 128], P('tensor', 'dp')
- down_grad: bfloat16 [32, 64, 128, 128], P('tensor', 'dp')
Inputs may be any that keep to these rules, and one draw needn't show every extreme that they name: `up_mask`: each column strip of 4 block columns holds exactly 64 ones. `down_mask`: the rows owned by one device hold exactly 64 ones together. `down_owner`: every device owns exactly 4 block rows.
All inputs are finite; a program needn't handle non-finite values.
Results may differ from a plain program's by a relative error of at most 0.022.
Values may be sent and summed in bfloat16 or wider, within the bound.
No kernel may reach another device: no remote copies, remote signals or barrier semaphores. Data moves between devices by JAX's collectives and lax.ppermute only.
A program may use at most 128 MiB of HBM per device.

v0:
```python
import jax
import jax.numpy as jnp
from jax import lax
from jax.sharding import PartitionSpec as P


def kept_positions(marked, total):
    marked = marked.reshape(-1).astype(jnp.int32)
    running = jnp.cumsum(marked) - 1
    target = jnp.where(marked > 0, running, total)
    indices = jnp.arange(marked.shape[0], dtype=jnp.int32)
    return jnp.zeros((total,), jnp.int32).at[target].set(indices, mode="drop")


def one_hot(indices, total):
    return (indices[:, None] == jnp.arange(total, dtype=jnp.int32)[None, :]).astype(jnp.float32)


def row_slots(down_owner, devices):
    marks = (down_owner[:, None] == jnp.arange(devices, dtype=jnp.int32)[None, :]).astype(jnp.int32)
    earlier = jnp.cumsum(marks, axis=0) - marks
    return jnp.sum(earlier * marks, axis=1)


def picker(wanted, block, current, segment):
    block_count = segment.shape[1] // block
    inside = (wanted >= 0) & (wanted < block_count)
    shaped = segment.reshape(segment.shape[0], block_count, block)
    chosen = jnp.take(shaped, jnp.clip(wanted, 0, block_count - 1), axis=1)
    return jnp.where(inside[None, :, None], chosen, current)


def shards(tokens, gate_pre, up_blocks, up_mask, down_blocks, down_mask, down_owner, cotangent):
    devices = lax.axis_size("tensor")
    position = lax.axis_index("tensor")
    token_count = tokens.shape[0]
    blocks_wide = up_mask.shape[0]
    strip_size = up_mask.shape[1]
    block = up_blocks.shape[2]
    kept_up = up_blocks.shape[1]
    kept_down = down_blocks.shape[1]
    model_width = blocks_wide * block
    highest = lax.Precision.HIGHEST
    x_full, dy_full = (
        lax.all_gather(tokens, "tensor", axis=1, tiled=True),
        lax.all_gather(cotangent, "tensor", axis=1, tiled=True),
    )
    token_blocks = x_full.reshape(token_count, blocks_wide, block)
    cot_blocks = dy_full.reshape(token_count, blocks_wide, block)
    w_up = up_blocks[0]
    w_down = down_blocks[0]
    up_pos = kept_positions(up_mask, kept_up)
    up_rows = up_pos // strip_size
    up_cols = up_pos % strip_size
    token_chosen = jnp.take(token_blocks, up_rows, axis=1)
    product = jnp.einsum("nkb,kbc->nkc", token_chosen, w_up, preferred_element_type=jnp.float32)
    up_val = jnp.einsum("nkc,ks->nsc", product, one_hot(up_cols, strip_size), precision=highest)
    gate_val = gate_pre.reshape(token_count, strip_size, block).astype(jnp.float32)
    sigmoid_gate = jax.nn.sigmoid(gate_val)
    activated = gate_val * sigmoid_gate
    hidden = (activated * up_val).astype(jnp.bfloat16).reshape(token_count, strip_size * block)
    my_rows = kept_positions(down_owner == position, strip_size)
    owned_mask = jnp.take(down_mask, my_rows, axis=0)
    down_pos = kept_positions(owned_mask, kept_down)
    slots = down_pos // blocks_wide
    down_cols = down_pos % blocks_wide
    empty = jnp.zeros((token_count, strip_size, block), jnp.bfloat16)
    hidden_owned = picker(
        my_rows, block, empty, lax.all_gather(hidden, "tensor", axis=1, tiled=True)
    )
    h_chosen = jnp.take(hidden_owned, slots, axis=1)
    product = jnp.einsum("nkb,kbc->nkc", h_chosen, w_down, preferred_element_type=jnp.float32)
    out_part = jnp.einsum(
        "nkc,kj->njc", product, one_hot(down_cols, blocks_wide), precision=highest
    )
    out_part = out_part.astype(jnp.bfloat16).reshape(1, token_count, model_width)
    dy_chosen = jnp.take(cot_blocks, down_cols, axis=1)
    down_term = jnp.einsum("nkb,nkc->kbc", h_chosen, dy_chosen, preferred_element_type=jnp.float32)[
        None
    ]
    backward = jnp.einsum("nkc,kbc->nkb", dy_chosen, w_down, preferred_element_type=jnp.float32)
    dh_owned = jnp.einsum("nkb,ka->nab", backward, one_hot(slots, strip_size), precision=highest)
    dh_owned = dh_owned.astype(jnp.bfloat16).reshape(token_count, strip_size * block)
    home_index = down_owner * strip_size + row_slots(down_owner, devices)
    targets = position * strip_size + jnp.arange(strip_size, dtype=jnp.int32)
    wanted = jnp.take(home_index, targets)
    hidden_grad = picker(
        wanted, block, empty, lax.all_gather(dh_owned, "tensor", axis=1, tiled=True)
    )
    dh_float = hidden_grad.astype(jnp.float32)
    gate_grad = (dh_float * up_val * sigmoid_gate * (1.0 + gate_val * (1.0 - sigmoid_gate))).astype(
        jnp.bfloat16
    )
    gate_grad = gate_grad.reshape(token_count, strip_size * block)
    up_act_grad = (dh_float * activated).astype(jnp.bfloat16)
    du_chosen = jnp.take(up_act_grad, up_cols, axis=1)
    product = jnp.einsum("nkc,kbc->nkb", du_chosen, w_up, preferred_element_type=jnp.float32)
    in_part = jnp.einsum("nkb,kr->nrb", product, one_hot(up_rows, blocks_wide), precision=highest)
    in_part = in_part.astype(jnp.bfloat16).reshape(1, token_count, model_width)
    up_term = jnp.einsum(
        "nkb,nkc->kbc", token_chosen, du_chosen, preferred_element_type=jnp.float32
    )[None]
    out_pieces, in_pieces = (
        lax.all_to_all(out_part, "tensor", split_axis=2, concat_axis=0, tiled=True),
        lax.all_to_all(in_part, "tensor", split_axis=2, concat_axis=0, tiled=True),
    )
    mixed = jnp.sum(out_pieces.astype(jnp.float32), axis=0).astype(jnp.bfloat16)
    input_grad = jnp.sum(in_pieces.astype(jnp.float32), axis=0).astype(jnp.bfloat16)
    up_sum, down_sum = (
        lax.psum_scatter(
            up_term.astype(jnp.bfloat16), "dp", scatter_dimension=1, tiled=True
        ).astype(jnp.float32),
        lax.psum_scatter(
            down_term.astype(jnp.bfloat16), "dp", scatter_dimension=1, tiled=True
        ).astype(jnp.float32),
    )
    up_grad = up_sum.astype(jnp.bfloat16)
    down_grad = down_sum.astype(jnp.bfloat16)
    return (mixed, input_grad, gate_grad, up_grad, down_grad)


def solution(mesh):
    placed = (
        P("dp", "tensor"),
        P("dp", "tensor"),
        P("tensor", None, None, None),
        P(None, "tensor"),
        P("tensor", None, None, None),
        P(),
        P(),
        P("dp", "tensor"),
    )
    return jax.shard_map(
        shards,
        mesh=mesh,
        in_specs=placed,
        out_specs=(
            P("dp", "tensor"),
            P("dp", "tensor"),
            P("dp", "tensor"),
            P("tensor", "dp", None, None),
            P("tensor", "dp", None, None),
        ),
        check_vma=False,
    )
```

profile of v0, /device:TPU:2, one launch (start us, length us, event | category | flops | bytes accessed | tf_op | source)
XLA Modules:
  0.0 517.0 jit_solution(11576796951660111175)
XLA Ops:
  18.4 79.6 %all-gather.9.cloned.1.call-done = bf16[128,4096]{0,1:T(8,128)(2,1)} async-done(((bf16[128,128]{0,1:T(8,128)(2,1)}), bf16[128,4096]{0,1:T(8,128)(2,1)}) %all-gather.9.cloned.1.call-update) | async-done | bytes 1048592 | tf_op jit(solution)/shard_map/all_gather | solution.py:46
  101.8 3.8 convolution_bitcast_fusion.1
  105.7 3.8 fusion.48
  115.2 66.1 %all-gather.5.cloned.1.call-done = bf16[128,4096]{0,1:T(8,128)(2,1)} async-done(((bf16[128,128]{0,1:T(8,128)(2,1)}), bf16[128,4096]{0,1:T(8,128)(2,1)}) %all-gather.5.cloned.1.call-update) | async-done | bytes 1048592 | tf_op jit(solution)/shard_map/all_gather | solution.py:45
  185.0 4.3 convolution_bitcast_fusion.3
  189.4 80.9 %all-gather.11.cloned.1.call-done = bf16[128,16384]{0,1:T(8,128)(2,1)} async-done(((bf16[128,512]{0,1:T(8,128)(2,1)}), bf16[128,16384]{0,1:T(8,128)(2,1)}) %all-gather.11.cloned.1.call-update) | async-done | bytes 4194320 | tf_op jit(solution)/shard_map/all_gather | solution.py:88
  270.3 6.4 %copy.134 = bf16[128,128,128]{2,0,1:T(8,128)(2,1)} copy(bf16[128,128,128]{0,2,1:T(8,128)(2,1)} %bitcast.106) | data formatting | bytes 8388608 | tf_op jit(solution)/shard_map/reshape | solution.py:28
  276.7 2.8 gather_fusion.6
  279.4 6.0 %fusion.54 = (bf16[128,4,128]{2,1,0:T(4,128)(2,1)S(1)}, bf16[128,4,128]{2,1,0:T(4,128)(2,1)S(1)}, bf16[128,4,128]{2,1,0:T(4,128)(2,1)S(1)}) fusion(f32[128,4,128]{2,1,0:T(4,128)S(1)} %reshape.234, bf16[4,128,128]{2,1,0:T(8,128)(2,1)S(1)} %gather_fusion.6, pred[4]{0:T(512)(128)(4,1)S(1)} %copy-done.17, pred[4]{0:T(512)(128)(4,1)S(1)} %copy-done.16, ...), kind=kOutput, calls=%fused_computation.55 | convolution fusion | flops 51511552 | bytes 4981000 | tf_op jit(solution)/shard_map/nkc,ks->nsc/dot_general | solution.py:57
  288.6 4.6 convert_bitcast_fusion.1
  293.9 5.2 %convolution_bitcast_fusion = f32[128,64,128]{2,0,1:T(8,128)} fusion(bf16[1,64,128,128]{3,2,1,0:T(8,128)(2,1)S(1)} %copy-done, bf16[64,128,128]{2,1,0:T(8,128)(2,1)} %gather_fusion.7, pred[64]{0:T(512)(128)(4,1)S(1)} %copy-done.6), kind=kOutput, calls=%fused_computation.19 | convolution fusion | flops 269484032 | bytes 8388672 | tf_op jit(solution)/shard_map/nkc,kbc->nkb/dot_general | solution.py:97
  299.1 72.1 %all-gather.7.cloned.1.call-done = bf16[128,16384]{0,1:T(8,128)(2,1)} async-done(((bf16[128,512]{0,1:T(8,128)(2,1)}), bf16[128,16384]{0,1:T(8,128)(2,1)}) %all-gather.7.cloned.1.call-update) | async-done | bytes 4194320 | tf_op jit(solution)/shard_map/all_gather | solution.py:69
  371.2 6.5 %copy.125 = bf16[128,128,128]{2,0,1:T(8,128)(2,1)} copy(bf16[128,128,128]{0,2,1:T(8,128)(2,1)} %bitcast.107) | data formatting | bytes 8388608 | tf_op jit(solution)/shard_map/reshape | solution.py:28
  382.8 4.6 convert_bitcast_fusion
  387.9 6.1 %fusion.36 = bf16[128,32,128]{2,1,0:T(8,128)(2,1)S(1)} fusion(f32[128,64,128]{2,0,1:T(8,128)} %convolution_bitcast_fusion, s32[64]{0:T(128)S(1)} %copy-done.14), kind=kOutput, calls=%fused_computation.45 | convolution fusion | flops 403179520 | bytes 5243136 | tf_op jit(solution)/shard_map/nkb,kr->nrb/dot_general | solution.py:98
  394.5 2.8 copy.138
  397.9 22.4 %reduce.15 = bf16[4096,128]{1,0:T(8,128)(2,1)S(1)} reduce(bf16[4096,1,128]{2,1,0:T(2,128)(2,1)S(1)} %bitcast.102, bf16[]{:T(256)} %broadcast.484), dimensions={1}, to_apply=%bitcast.95.reduce_sub_computation | reduce | bytes 2097154
  421.4 7.0 %all-to-all-start.1 = ((bf16[32,2,8192]{2,1,0:T(2,128)(2,1)}), bf16[32,2,8192]{2,1,0:T(2,128)(2,1)S(1)}, u32[]{:S(2)}, u32[]{:S(2)}) async-start(bf16[32,2,8192]{2,1,0:T(2,128)(2,1)} %reshape.359), calls=%async_computation.1 | async-start | bytes 2097152 | tf_op jit(solution)/shard_map/all_to_all | solution.py:105
  430.8 4.1 fusion.39
  436.2 5.0 copy.129
  441.2 23.4 %reduce.14 = bf16[4096,128]{1,0:T(8,128)(2,1)} reduce(bf16[4096,1,128]{2,1,0:T(2,128)(2,1)S(1)} %bitcast.103, bf16[]{:T(256)} %broadcast.484), dimensions={1}, to_apply=%bitcast.93.reduce_sub_computation | reduce | bytes 2097154
  466.7 9.8 %all-to-all-start = ((bf16[32,2,8192]{2,1,0:T(2,128)(2,1)}), bf16[32,2,8192]{2,1,0:T(2,128)(2,1)}, u32[]{:S(2)}, u32[]{:S(2)}) async-start(bf16[32,2,8192]{2,1,0:T(2,128)(2,1)} %reshape.357), calls=%async_computation | async-start | bytes 2097152 | tf_op jit(solution)/shard_map/all_to_all | solution.py:104
  479.3 22.0 %all-to-all-done = bf16[32,2,8192]{2,1,0:T(2,128)(2,1)} async-done(((bf16[32,2,8192]{2,1,0:T(2,128)(2,1)}), bf16[32,2,8192]{2,1,0:T(2,128)(2,1)}, u32[]{:S(2)}, u32[]{:S(2)}) %all-to-all-start) | async-done | bytes 1048608 | tf_op jit(solution)/shard_map/all_to_all | solution.py:104
  501.3 5.8 %reshape.358 = bf16[4096,1,128]{2,1,0:T(2,128)(2,1)} reshape(bf16[32,2,8192]{2,1,0:T(2,128)(2,1)} %all-to-all-done) | data formatting | bytes 2097152
  (124 shorter events, 47.1 us)
Async XLA Ops:
  7.2 177.9 %copy-start = (bf16[1,64,128,128]{3,2,1,0:T(8,128)(2,1)S(1)}, bf16[1,64,128,128]{3,2,1,0:T(8,128)(2,1)}, u32[]{:S(2)}) copy-start(bf16[1,64,128,128]{3,2,1,0:T(8,128)(2,1)} %param.16) | copy-start | bytes 6291460
  7.2 90.8 %all-gather.9.cloned.1.call-start = ((), (), s32[]{:S(2)}) async-start(), calls=%async_computation.6 | async-start | bytes 1081344 | tf_op jit(solution)/shard_map/all_gather | solution.py:46
  8.9 172.4 %all-gather.5.cloned.1.call-start = ((), (), s32[]{:S(2)}) async-start(), calls=%async_computation.4 | async-start | bytes 1081344 | tf_op jit(solution)/shard_map/all_gather | solution.py:45
  10.4 259.9 %all-gather.11.cloned.1.call-start = ((), (), s32[]{:S(2)}) async-start(), calls=%async_computation.7 | async-start | bytes 4325376 | tf_op jit(solution)/shard_map/all_gather | solution.py:88
  18.3 83.5 %copy-start.11 = (s32[64]{0:T(128)}, s32[64]{0:T(128)S(1)}, u32[]{:S(2)}) copy-start(s32[64]{0:T(128)S(1)} %get-tuple-element.20) | copy-start | bytes 772
  18.3 87.3 %copy-start.4 = (s32[64]{0:T(128)}, s32[64]{0:T(128)S(1)}, u32[]{:S(2)}) copy-start(s32[64]{0:T(128)S(1)} %get-tuple-element.33) | copy-start | bytes 772
  105.6 4.7 copy-start.9
  105.7 5.0 copy-start.3
  110.3 260.9 %all-gather.7.cloned.1.call-start = ((), (), s32[]{:S(2)}) async-start(), calls=%async_computation.5 | async-start | bytes 4325376 | tf_op jit(solution)/shard_map/all_gather | solution.py:69
  114.6 70.4 %copy-start.7 = (pred[64]{0:T(512)(128)(4,1)}, pred[64]{0:T(512)(128)(4,1)S(1)}, u32[]{:S(2)}) copy-start(pred[64]{0:T(512)(128)(4,1)S(1)} %get-tuple-element.38) | copy-start | bytes 196
  270.3 9.2 %copy-start.15 = (s32[64]{0:T(128)S(1)}, s32[64]{0:T(128)}, u32[]{:S(2)}) copy-start(s32[64]{0:T(128)} %get-tuple-element.14) | copy-start | bytes 772
  270.3 9.2 %copy-start.16 = (pred[4]{0:T(512)(128)(4,1)S(1)}, pred[4]{0:T(512)(128)(4,1)}, u32[]{:S(2)}) copy-start(pred[4]{0:T(512)(128)(4,1)} %get-tuple-element.15) | copy-start | bytes 16
  270.3 9.2 %copy-start.17 = (pred[4]{0:T(512)(128)(4,1)S(1)}, pred[4]{0:T(512)(128)(4,1)}, u32[]{:S(2)}) copy-start(pred[4]{0:T(512)(128)(4,1)} %get-tuple-element.17) | copy-start | bytes 16
  286.3 223.6 %reduce-scatter.3.cloned.1.call-start = ((), (), s32[]{:S(2)}) async-start(), calls=%async_computation.8 | async-start | bytes 2228224 | tf_op jit(solution)/shard_map/reduce_scatter | solution.py:110
  286.4 2.2 copy-start.6
  286.4 2.2 copy-start.8
  293.2 0.7 copy-start.10
  293.2 0.7 copy-start.5
  293.2 216.7 %reduce-scatter.5.cloned.1.call-start = ((), (), s32[]{:S(2)}) async-start(), calls=%async_computation.9 | async-start | bytes 2228224 | tf_op jit(solution)/shard_map/reduce_scatter | solution.py:113
  420.2 8.2 %copy-start.2 = (bf16[64,128,128]{2,1,0:T(8,128)(2,1)S(1)}, bf16[64,128,128]{2,1,0:T(8,128)(2,1)}, u32[]{:S(2)}) copy-start(bf16[64,128,128]{2,1,0:T(8,128)(2,1)} %gather_fusion.4) | copy-start | bytes 6291460
  421.4 45.4 %all-to-all-start.1 = ((bf16[32,2,8192]{2,1,0:T(2,128)(2,1)}), bf16[32,2,8192]{2,1,0:T(2,128)(2,1)S(1)}, u32[]{:S(2)}, u32[]{:S(2)}) async-start(bf16[32,2,8192]{2,1,0:T(2,128)(2,1)} %reshape.359), calls=%async_computation.1 | async-start | bytes 2097152 | tf_op jit(solution)/shard_map/all_to_all | solution.py:105
  428.4 2.4 copy-start.12
  466.7 34.6 %all-to-all-start = ((bf16[32,2,8192]{2,1,0:T(2,128)(2,1)}), bf16[32,2,8192]{2,1,0:T(2,128)(2,1)}, u32[]{:S(2)}, u32[]{:S(2)}) async-start(bf16[32,2,8192]{2,1,0:T(2,128)(2,1)} %reshape.357), calls=%async_computation | async-start | bytes 2097152 | tf_op jit(solution)/shard_map/all_to_all | solution.py:104
  507.1 2.8 copy-start.1
  (2 other events, 1.1 us)
Sparse Core Ops, SparseCore 0:
  11.8 86.1 all-gather.8
  101.7 79.5 all-gather.4
  185.0 85.2 all-gather.10
  286.4 84.7 all-gather.6
  374.4 59.0 reduce-scatter.2
  436.8 61.4 reduce-scatter.4
where the time goes:
time: 525 us; the launch traced here: 517 us
  waiting for transfers between devices  321 us (61%)
  local copies, waits for them, and re-layouts  67 us (13%)
  other arithmetic  52.4 us (10%)
  matrix products  44.8 us (9%)
  starting transfers between devices  17.1 us (3%)
  between operations  14.8 us (3%)
    all_gather x1, waiting for transfers between devices, shards(): lax.all_gather(dh_owned, 'tensor', axis=1, tiled=True)  80.9 us
    all_gather x1, waiting for transfers between devices, shards(): lax.all_gather(cotangent, 'tensor', axis=1, tiled=True)  79.6 us
    all_gather x1, waiting for transfers between devices, shards(): lax.all_gather(hidden, 'tensor', axis=1, tiled=True)  72.1 us
    all_gather x1, waiting for transfers between devices, shards(): lax.all_gather(tokens, 'tensor', axis=1, tiled=True)  66.1 us
    unnamed x2, other arithmetic  45.8 us
    all_to_all x1, waiting for transfers between devices, shards(): lax.all_to_all(out_part, 'tensor', split_axis=2, concat_axis=0, tiled=True)  22 us
    unnamed x50, local copies, waits for them, and re-layouts  20.5 us
    reshape x2, local copies, waits for them, and re-layouts, picker(): shaped = segment.reshape(segment.shape[0], block_count, block)  12.9 us
  transfers between devices with their start and end apart: 8, of which 5 were waited for; matrix products, arithmetic and copies ran while one was open for 28% of the time, Pallas kernels for 0%

commit v1 on v0

--- a/solution.py
+++ b/solution.py
@@ -2,6 +2,29 @@
 import jax.numpy as jnp
 from jax import lax
 from jax.sharding import PartitionSpec as P
+
+
+def lines_tell(panel, on_dim):
+    opened = list(panel.shape[1:])
+    opened[on_dim] *= panel.shape[0]
+    return jnp.moveaxis(panel, 0, on_dim).reshape(opened)
+
+
+def try_all_steps_all_on(m, lane_axis):
+    base_arr, piece_now = (lax.axis_size(lane_axis), lax.axis_index(lane_axis))
+    x_now, left_arr = (m[None], 1)
+    while left_arr < base_arr:
+        moved = lax.ppermute(x_now, lane_axis, [(no, no ^ left_arr) for no in range(base_arr)])
+        mixed_arr = piece_now & left_arr == 0
+        x_now = jnp.concatenate(
+            [jnp.where(mixed_arr, x_now, moved), jnp.where(mixed_arr, moved, x_now)]
+        )
+        left_arr *= 2
+    return x_now
+
+
+def push_sources_all_over_axis(local_values, arr_in, which_dim):
+    return lines_tell(try_all_steps_all_on(local_values, arr_in), which_dim)
 
 
 def kept_positions(marked, total):
@@ -42,7 +65,7 @@
     model_width = blocks_wide * block
     highest = lax.Precision.HIGHEST
     x_full, dy_full = (
-        lax.all_gather(tokens, "tensor", axis=1, tiled=True),
+        push_sources_all_over_axis(tokens, "tensor", 1),
         lax.all_gather(cotangent, "tensor", axis=1, tiled=True),
     )
     token_blocks = x_full.reshape(token_count, blocks_wide, block)

time: 525 us -> 459 us (0.87)
  waiting for transfers between devices: 321 us -> 240 us
  starting transfers between devices: 17.1 us -> 36 us
    all_gather x1 -> x0, waiting for transfers between devices: 66.1 us -> none  [shards(): lax.all_gather(tokens, 'tensor', axis=1, tiled=True)]
    all_gather x1, waiting for transfers between devices: 80.9 us -> 19.5 us  [shards(): lax.all_gather(dh_owned, 'tensor', axis=1, tiled=True)]
    ppermute x0 -> x5, waiting for transfers between devices: none -> 44.8 us  [try_all_steps_all_on(): lax.ppermute(x_now, lane_axis, [(no, no ^ left_arr) for no in range(base_...]
    ppermute x0 -> x5, starting transfers between devices: none -> 18.9 us  [try_all_steps_all_on(): lax.ppermute(x_now, lane_axis, [(no, no ^ left_arr) for no in range(base_...]
    unnamed x50 -> x51, local copies, waits for them, and re-layouts: 20.5 us -> 18.5 us
  transfers between devices with their start and end apart: 8 -> 12, of which waited for: 5 -> 9; matrix products, arithmetic and copies ran while one was open for 28% -> 29% of each run, Pallas kernels for 0% -> 0%
where the time goes in v1:
time: 459 us; the launch traced here: 451 us
  waiting for transfers between devices  240 us (52%)
  local copies, waits for them, and re-layouts  62.9 us (14%)
  other arithmetic  52.7 us (11%)
  matrix products  44.9 us (10%)
  starting transfers between devices  36 us (8%)
  between operations  14.6 us (3%)
    all_gather x1, waiting for transfers between devices, shards(): lax.all_gather(cotangent, 'tensor', axis=1, tiled=True)  81.1 us
    all_gather x1, waiting for transfers between devices, shards(): lax.all_gather(hidden, 'tensor', axis=1, tiled=True)  72.4 us
    unnamed x2, other arithmetic  45.8 us
    ppermute x5, waiting for transfers between devices, try_all_steps_all_on(): lax.ppermute(x_now, lane_axis, [(no, no ^ left_arr) for no in range(base_...  44.8 us
    all_to_all x1, waiting for transfers between devices, shards(): lax.all_to_all(out_part, 'tensor', split_axis=2, concat_axis=0, tiled=True)  22 us
    all_gather x1, waiting for transfers between devices, shards(): lax.all_gather(dh_owned, 'tensor', axis=1, tiled=True)  19.5 us
    ppermute x5, starting transfers between devices, try_all_steps_all_on(): lax.ppermute(x_now, lane_axis, [(no, no ^ left_arr) for no in range(base_...  18.9 us
    unnamed x51, local copies, waits for them, and re-layouts  18.5 us
  transfers between devices with their start and end apart: 12, of which 9 were waited for; matrix products, arithmetic and copies ran while one was open for 29% of the time, Pallas kernels for 0%

profile of v1, /device:TPU:2, one launch (start us, length us, event | category | flops | bytes accessed | tf_op | source)
XLA Modules:
  0.0 451.1 jit_solution(6329616484222681552)
XLA Ops:
  16.8 81.1 %all-gather.6.cloned.1.call-done = bf16[128,4096]{0,1:T(8,128)(2,1)} async-done(((bf16[128,128]{0,1:T(8,128)(2,1)}), bf16[128,4096]{0,1:T(8,128)(2,1)}) %all-gather.6.cloned.1.call-update) | async-done | bytes 1048592 | tf_op jit(solution)/shard_map/all_gather | solution.py:69
  127.3 4.6 %collective-permute-done.2 = bf16[4,128,128]{2,1,0:T(8,128)(2,1)S(1)} collective-permute-done((bf16[4,128,128]{2,1,0:T(8,128)(2,1)S(1)}, bf16[4,128,128]{2,1,0:T(8,128)(2,1)S(1)}, u32[]{:S(2)}, u32[]{:S(2)}) %collective-permute-start.2) | collective-permute-done | bytes 131104 | tf_op jit(solution)/shard_map/ppermute | solution.py:17
  132.0 4.0 collective-permute-start.3
  136.1 21.3 %collective-permute-done.3 = bf16[8,128,128]{2,1,0:T(8,128)(2,1)S(1)} collective-permute-done((bf16[8,128,128]{2,1,0:T(8,128)(2,1)S(1)}, bf16[8,128,128]{2,1,0:T(8,128)(2,1)S(1)}, u32[]{:S(2)}, u32[]{:S(2)}) %collective-permute-start.3) | collective-permute-done | bytes 262176 | tf_op jit(solution)/shard_map/ppermute | solution.py:17
  157.5 5.6 %collective-permute-start.4 = (bf16[16,128,128]{2,1,0:T(8,128)(2,1)S(1)}, bf16[16,128,128]{2,1,0:T(8,128)(2,1)S(1)}, u32[]{:S(2)}, u32[]{:S(2)}) collective-permute-start(bf16[16,128,128]{2,1,0:T(8,128)(2,1)S(1)} %pad_maximum_fusion), channel_id=1, source_target_pairs={{0,16},{1,17},{2,18},{3,19},{4,20},{5,21},{6,22},{7,23},{8,24},{9,... | collective-permute-start | bytes 1572872 | tf_op jit(solution)/shard_map/ppermute | solution.py:17
  164.2 13.9 %collective-permute-done.4 = bf16[16,128,128]{2,1,0:T(8,128)(2,1)S(1)} collective-permute-done((bf16[16,128,128]{2,1,0:T(8,128)(2,1)S(1)}, bf16[16,128,128]{2,1,0:T(8,128)(2,1)S(1)}, u32[]{:S(2)}, u32[]{:S(2)}) %collective-permute-start.4) | collective-permute-done | bytes 524320 | tf_op jit(solution)/shard_map/ppermute | solution.py:17
  180.5 4.4 convolution_bitcast_fusion.3
  184.9 19.5 %all-gather.8.cloned.1.call-done = bf16[128,16384]{0,1:T(8,128)(2,1)} async-done(((bf16[128,512]{0,1:T(8,128)(2,1)}), bf16[128,16384]{0,1:T(8,128)(2,1)}) %all-gather.8.cloned.1.call-update) | async-done | bytes 4194320 | tf_op jit(solution)/shard_map/all_gather | solution.py:111
  204.4 6.4 %copy.127 = bf16[128,128,128]{2,0,1:T(8,128)(2,1)} copy(bf16[128,128,128]{0,2,1:T(8,128)(2,1)} %bitcast.113) | data formatting | bytes 8388608 | tf_op jit(solution)/shard_map/reshape | solution.py:51
  213.6 6.0 %fusion.54 = (bf16[128,4,128]{2,1,0:T(4,128)(2,1)S(1)}, bf16[128,4,128]{2,1,0:T(4,128)(2,1)S(1)}, bf16[128,4,128]{2,1,0:T(4,128)(2,1)S(1)}) fusion(f32[128,4,128]{2,1,0:T(4,128)S(1)} %reshape.230, bf16[4,128,128]{2,1,0:T(8,128)(2,1)S(1)} %gather_fusion.6, pred[4]{0:T(512)(128)(4,1)S(1)} %copy-done.18, pred[4]{0:T(512)(128)(4,1)S(1)} %copy-done.17, ...), kind=kOutput, calls=%fused_computation.59 | convolution fusion | flops 51511552 | bytes 4981000 | tf_op jit(solution)/shard_map/nkc,ks->nsc/dot_general | solution.py:80
  222.8 4.6 %convert_bitcast_fusion.1 = bf16[1,64,128,128]{3,2,1,0:T(8,128)(2,1)} fusion(bf16[64,128,128]{2,1,0:T(8,128)(2,1)} %gather_fusion.2, pred[64]{0:T(512)(128)(4,1)S(1)} %copy-done.9, bf16[64,128,128]{2,1,0:T(8,128)(2,1)} %gather_fusion.7, pred[64]{0:T(512)(128)(4,1)S(1)} %copy-done.7), kind=kOutput, calls=%fused_computation.38 | convolution fusion | flops 271581184 | bytes 6291584 | tf_op jit(solution)/shard_map/nkb,nkc->kbc/dot_general | solution.py:123
  228.0 5.2 %convolution_bitcast_fusion = f32[128,64,128]{2,0,1:T(8,128)} fusion(bf16[1,64,128,128]{3,2,1,0:T(8,128)(2,1)S(1)} %copy-done, bf16[64,128,128]{2,1,0:T(8,128)(2,1)} %gather_fusion.7, pred[64]{0:T(512)(128)(4,1)S(1)} %copy-done.7), kind=kOutput, calls=%fused_computation.19 | convolution fusion | flops 269484032 | bytes 8388672 | tf_op jit(solution)/shard_map/nkc,kbc->nkb/dot_general | solution.py:120
  233.2 72.4 %all-gather.4.cloned.1.call-done = bf16[128,16384]{0,1:T(8,128)(2,1)} async-done(((bf16[128,512]{0,1:T(8,128)(2,1)}), bf16[128,16384]{0,1:T(8,128)(2,1)}) %all-gather.4.cloned.1.call-update) | async-done | bytes 4194320 | tf_op jit(solution)/shard_map/all_gather | solution.py:92
  305.6 6.5 %copy.118 = bf16[128,128,128]{2,0,1:T(8,128)(2,1)} copy(bf16[128,128,128]{0,2,1:T(8,128)(2,1)} %bitcast.114) | data formatting | bytes 8388608 | tf_op jit(solution)/shard_map/reshape | solution.py:51
  317.2 4.6 %convert_bitcast_fusion = bf16[1,64,128,128]{3,2,1,0:T(8,128)(2,1)} fusion(bf16[64,128,128]{2,1,0:T(8,128)(2,1)} %gather_fusion.4, pred[64]{0:T(512)(128)(4,1)S(1)} %get-tuple-element.42, bf16[64,128,128]{2,1,0:T(8,128)(2,1)} %gather_fusion.5, pred[64]{0:T(512)(128)(4,1)S(1)} %get-tuple-element.19), kind=kOutput, calls=%fused_computation.37 | convolution fusion | flops 271581184 | bytes 6291584 | tf_op jit(solution)/shard_map/nkb,nkc->kbc/dot_general | solution.py:101
  322.4 6.1 %fusion.36 = bf16[128,32,128]{2,1,0:T(8,128)(2,1)S(1)} fusion(f32[128,64,128]{2,0,1:T(8,128)} %convolution_bitcast_fusion, s32[64]{0:T(128)S(1)} %copy-done.15), kind=kOutput, calls=%fused_computation.45 | convolution fusion | flops 403179520 | bytes 5243136 | tf_op jit(solution)/shard_map/nkb,kr->nrb/dot_general | solution.py:121
  332.3 22.4 %reduce.15 = bf16[4096,128]{1,0:T(8,128)(2,1)S(1)} reduce(bf16[4096,1,128]{2,1,0:T(2,128)(2,1)S(1)} %bitcast.109, bf16[]{:T(256)} %broadcast.484), dimensions={1}, to_apply=%bitcast.99.reduce_sub_computation | reduce | bytes 2097154
  355.8 7.0 %all-to-all-start.1 = ((bf16[32,2,8192]{2,1,0:T(2,128)(2,1)}), bf16[32,2,8192]{2,1,0:T(2,128)(2,1)S(1)}, u32[]{:S(2)}, u32[]{:S(2)}) async-start(bf16[32,2,8192]{2,1,0:T(2,128)(2,1)} %reshape.355), calls=%async_computation.1 | async-start | bytes 2097152 | tf_op jit(solution)/shard_map/all_to_all | solution.py:128
  365.3 4.1 fusion.39
  370.6 5.0 %copy.122 = bf16[1,128,4096]{1,0,2:T(2,128)(2,1)S(1)} copy(bf16[1,128,4096]{2,1,0:T(8,128)(2,1)} %reshape.224) | data formatting | bytes 2097152 | tf_op jit(solution)/shard_map/reshape | solution.py:99
  375.7 23.4 %reduce.14 = bf16[4096,128]{1,0:T(8,128)(2,1)} reduce(bf16[4096,1,128]{2,1,0:T(2,128)(2,1)S(1)} %bitcast.110, bf16[]{:T(256)} %broadcast.484), dimensions={1}, to_apply=%bitcast.97.reduce_sub_computation | reduce | bytes 2097154
  401.2 9.8 %all-to-all-start = ((bf16[32,2,8192]{2,1,0:T(2,128)(2,1)}), bf16[32,2,8192]{2,1,0:T(2,128)(2,1)}, u32[]{:S(2)}, u32[]{:S(2)}) async-start(bf16[32,2,8192]{2,1,0:T(2,128)(2,1)} %reshape.353), calls=%async_computation | async-start | bytes 2097152 | tf_op jit(solution)/shard_map/all_to_all | solution.py:127
  413.8 22.0 %all-to-all-done = bf16[32,2,8192]{2,1,0:T(2,128)(2,1)} async-done(((bf16[32,2,8192]{2,1,0:T(2,128)(2,1)}), bf16[32,2,8192]{2,1,0:T(2,128)(2,1)}, u32[]{:S(2)}, u32[]{:S(2)}) %all-to-all-start) | async-done | bytes 1048608 | tf_op jit(solution)/shard_map/all_to_all | solution.py:127
  435.8 5.7 %reshape.354 = bf16[4096,1,128]{2,1,0:T(2,128)(2,1)} reshape(bf16[32,2,8192]{2,1,0:T(2,128)(2,1)} %all-to-all-done) | data formatting | bytes 2097152
  (141 shorter events, 70.6 us)
Async XLA Ops:
  7.2 173.3 %copy-start = (bf16[1,64,128,128]{3,2,1,0:T(8,128)(2,1)S(1)}, bf16[1,64,128,128]{3,2,1,0:T(8,128)(2,1)}, u32[]{:S(2)}) copy-start(bf16[1,64,128,128]{3,2,1,0:T(8,128)(2,1)} %param.16) | copy-start | bytes 6291460
  7.2 90.8 %all-gather.6.cloned.1.call-start = ((), (), s32[]{:S(2)}) async-start(), calls=%async_computation.5 | async-start | bytes 1081344 | tf_op jit(solution)/shard_map/all_gather | solution.py:69
  8.9 195.6 %all-gather.8.cloned.1.call-start = ((), (), s32[]{:S(2)}) async-start(), calls=%async_computation.6 | async-start | bytes 4325376 | tf_op jit(solution)/shard_map/all_gather | solution.py:111
  16.8 85.0 %copy-start.12 = (s32[64]{0:T(128)}, s32[64]{0:T(128)S(1)}, u32[]{:S(2)}) copy-start(s32[64]{0:T(128)S(1)} %get-tuple-element.20) | copy-start | bytes 772
  16.8 88.8 %copy-start.5 = (s32[64]{0:T(128)}, s32[64]{0:T(128)S(1)}, u32[]{:S(2)}) copy-start(s32[64]{0:T(128)S(1)} %get-tuple-element.43) | copy-start | bytes 772
  105.6 4.7 %copy-start.4 = (bf16[128,128]{1,0:T(8,128)(2,1)S(1)}, bf16[128,128]{1,0:T(8,128)(2,1)}, u32[]{:S(2)}) copy-start(bf16[128,128]{1,0:T(8,128)(2,1)} %param.14) | copy-start | bytes 98308
  105.6 7.9 %copy-start.10 = (s32[32,4]{0,1:T(4,128)S(1)}, s32[32,4]{0,1:T(4,128)}, u32[]{:S(2)}) copy-start(s32[32,4]{0,1:T(4,128)} %param.17) | copy-start | bytes 1540
  105.6 8.3 %copy-start.3 = (bf16[128,512]{1,0:T(8,128)(2,1)S(1)}, bf16[128,512]{1,0:T(8,128)(2,1)}, u32[]{:S(2)}) copy-start(bf16[128,512]{1,0:T(8,128)(2,1)} %param.15) | copy-start | bytes 393220
  110.3 195.4 %all-gather.4.cloned.1.call-start = ((), (), s32[]{:S(2)}) async-start(), calls=%async_computation.4 | async-start | bytes 4325376 | tf_op jit(solution)/shard_map/all_gather | solution.py:92
  110.3 6.2 %collective-permute-start = (bf16[1,128,128]{2,1,0:T(8,128)(2,1)S(1)}, bf16[1,128,128]{2,1,0:T(8,128)(2,1)S(1)}, u32[]{:S(2)}, u32[]{:S(2)}) collective-permute-start(bf16[1,128,128]{2,1,0:T(8,128)(2,1)S(1)} %bitcast.120), channel_id=1, source_target_pairs={{0,1},{1,0},{2,3},{3,2},{4,5},{5,4},{6,7},{7,6},{8,9},{9,8},{10,11... | collective-permute-start | bytes 98312 | tf_op jit(solution)/shard_map/ppermute | solution.py:17
  116.5 7.7 %collective-permute-start.1 = (bf16[2,128,128]{2,1,0:T(8,128)(2,1)S(1)}, bf16[2,128,128]{2,1,0:T(8,128)(2,1)S(1)}, u32[]{:S(2)}, u32[]{:S(2)}) collective-permute-start(bf16[2,128,128]{2,1,0:T(8,128)(2,1)S(1)} %pad_maximum_fusion.3), channel_id=1, source_target_pairs={{0,2},{1,3},{2,0},{3,1},{4,6},{5,7},{6,4},{7,5},{8,10},{9,11},{10,... | collective-permute-start | bytes 196616 | tf_op jit(solution)/shard_map/ppermute | solution.py:17
  124.2 7.8 %collective-permute-start.2 = (bf16[4,128,128]{2,1,0:T(8,128)(2,1)S(1)}, bf16[4,128,128]{2,1,0:T(8,128)(2,1)S(1)}, u32[]{:S(2)}, u32[]{:S(2)}) collective-permute-start(bf16[4,128,128]{2,1,0:T(8,128)(2,1)S(1)} %pad_maximum_fusion.2), channel_id=1, source_target_pairs={{0,4},{1,5},{2,6},{3,7},{4,0},{5,1},{6,2},{7,3},{8,12},{9,13},{10,... | collective-permute-start | bytes 393224 | tf_op jit(solution)/shard_map/ppermute | solution.py:17
  127.3 8.7 %copy-start.14 = (s32[64]{0:T(128)}, s32[64]{0:T(128)S(1)}, u32[]{:S(2)}) copy-start(s32[64]{0:T(128)S(1)} %get-tuple-element.49) | copy-start | bytes 772
  127.3 53.1 %copy-start.8 = (pred[64]{0:T(512)(128)(4,1)}, pred[64]{0:T(512)(128)(4,1)S(1)}, u32[]{:S(2)}) copy-start(pred[64]{0:T(512)(128)(4,1)S(1)} %get-tuple-element.48) | copy-start | bytes 196
  132.0 25.4 %collective-permute-start.3 = (bf16[8,128,128]{2,1,0:T(8,128)(2,1)S(1)}, bf16[8,128,128]{2,1,0:T(8,128)(2,1)S(1)}, u32[]{:S(2)}, u32[]{:S(2)}) collective-permute-start(bf16[8,128,128]{2,1,0:T(8,128)(2,1)S(1)} %pad_maximum_fusion.1), channel_id=1, source_target_pairs={{0,8},{1,9},{2,10},{3,11},{4,12},{5,13},{6,14},{7,15},{8,0},{9,1},... | collective-permute-start | bytes 786440 | tf_op jit(solution)/shard_map/ppermute | solution.py:17
  157.5 20.6 %collective-permute-start.4 = (bf16[16,128,128]{2,1,0:T(8,128)(2,1)S(1)}, bf16[16,128,128]{2,1,0:T(8,128)(2,1)S(1)}, u32[]{:S(2)}, u32[]{:S(2)}) collective-permute-start(bf16[16,128,128]{2,1,0:T(8,128)(2,1)S(1)} %pad_maximum_fusion), channel_id=1, source_target_pairs={{0,16},{1,17},{2,18},{3,19},{4,20},{5,21},{6,22},{7,23},{8,24},{9,... | collective-permute-start | bytes 1572872 | tf_op jit(solution)/shard_map/ppermute | solution.py:17
  204.4 9.2 %copy-start.16 = (s32[64]{0:T(128)S(1)}, s32[64]{0:T(128)}, u32[]{:S(2)}) copy-start(s32[64]{0:T(128)} %get-tuple-element.14) | copy-start | bytes 772
  204.4 9.2 %copy-start.17 = (pred[4]{0:T(512)(128)(4,1)S(1)}, pred[4]{0:T(512)(128)(4,1)}, u32[]{:S(2)}) copy-start(pred[4]{0:T(512)(128)(4,1)} %get-tuple-element.15) | copy-start | bytes 16
  204.4 9.2 %copy-start.18 = (pred[4]{0:T(512)(128)(4,1)S(1)}, pred[4]{0:T(512)(128)(4,1)}, u32[]{:S(2)}) copy-start(pred[4]{0:T(512)(128)(4,1)} %get-tuple-element.17) | copy-start | bytes 16
  220.5 223.8 %reduce-scatter.3.cloned.1.call-start = ((), (), s32[]{:S(2)}) async-start(), calls=%async_computation.7 | async-start | bytes 2228224 | tf_op jit(solution)/shard_map/reduce_scatter | solution.py:133
  227.3 217.0 %reduce-scatter.5.cloned.1.call-start = ((), (), s32[]{:S(2)}) async-start(), calls=%async_computation.8 | async-start | bytes 2228224 | tf_op jit(solution)/shard_map/reduce_scatter | solution.py:136
  354.7 8.2 %copy-start.2 = (bf16[64,128,128]{2,1,0:T(8,128)(2,1)S(1)}, bf16[64,128,128]{2,1,0:T(8,128)(2,1)}, u32[]{:S(2)}) copy-start(bf16[64,128,128]{2,1,0:T(8,128)(2,1)} %gather_fusion.4) | copy-start | bytes 6291460
  355.8 45.4 %all-to-all-start.1 = ((bf16[32,2,8192]{2,1,0:T(2,128)(2,1)}), bf16[32,2,8192]{2,1,0:T(2,128)(2,1)S(1)}, u32[]{:S(2)}, u32[]{:S(2)}) async-start(bf16[32,2,8192]{2,1,0:T(2,128)(2,1)} %reshape.355), calls=%async_computation.1 | async-start | bytes 2097152 | tf_op jit(solution)/shard_map/all_to_all | solution.py:128
  401.2 34.6 %all-to-all-start = ((bf16[32,2,8192]{2,1,0:T(2,128)(2,1)}), bf16[32,2,8192]{2,1,0:T(2,128)(2,1)}, u32[]{:S(2)}, u32[]{:S(2)}) async-start(bf16[32,2,8192]{2,1,0:T(2,128)(2,1)} %reshape.353), calls=%async_computation | async-start | bytes 2097152 | tf_op jit(solution)/shard_map/all_to_all | solution.py:127
  (7 other events, 11.5 us)
Sparse Core Ops, SparseCore 0:
  11.8 86.1 all-gather.5
  110.4 94.0 all-gather.7
  220.6 84.9 all-gather.3
  308.9 59.0 reduce-scatter.2
  371.2 61.5 reduce-scatter.4
